TPU v7x, 32 devices: a whole 2x2x4 slice. The times are simulated.
32 devices in a mesh: groups: 2 (over x), section: 2 (over core), tensor: 8 (over z, y).
Axes of the slice: x: 2, y: 2, z: 4, core: 2. Of those that a mesh axis runs over, the one named last changes fastest.
Arguments:
- hidden: bfloat16 [2, 1024, 26624], P('section', 'groups', 'tensor'), parts along dimension 1, may hold values from -6 to 6
- down_weight: bfloat16 [2, 26624, 8192], P('section', 'tensor'), may hold values from -0.0546875 to 0.0546875
- residual: bfloat16 [2, 1024, 8192], P('section', 'groups', 'tensor'), parts along dimension 1, may hold values from -100 to 100
- norm_gain: float32 [2, 8192], P('section'), may hold values from 0.1 to 1.9
- qkv_weight: bfloat16 [2, 8192, 9216], P('section', None, 'tensor'), may hold values from -0.0625 to 0.0625
Outputs:
- received: bfloat16 [2, 1024, 8192], P('section', 'groups', 'tensor'), parts along dimension 1
- projected: bfloat16 [2, 1024, 9216], P('section', 'groups', 'tensor'), parts along dimension 1
There are 2 independent parts, one for each index of `groups`. A program takes and returns all parts, laid end to end along the dimension named above; an argument that names none is the same for every part. Nothing has to cross between parts.
All inputs are finite; a program needn't handle non-finite values.
Results may differ from a plain program's by a relative error of at most 0.0057.
Values may be sent and summed in bfloat16 or wider, within the bound.
A program may use at most 192 MiB of HBM per device.

v0:
```python
import jax
import jax.numpy as jnp
from jax import lax
from jax.sharding import PartitionSpec as P

D = 8192


epsilon = 1e-05


def shifted(value, axis, steps):
    count = lax.axis_size(axis)
    pairs = [(source, (source + steps) % count) for source in range(count)]
    return lax.ppermute(value, axis, pairs)


def normalize(floats, gain_part):
    square_sum = jnp.sum(floats * floats, axis=1, keepdims=True)
    scale_inv = lax.rsqrt(square_sum / D + epsilon)
    return (floats * scale_inv * gain_part[None, :]).astype(jnp.bfloat16)


def body(hidden, down_weight, residual, norm_gain, qkv_weight):
    hidden_local = hidden[0]
    down_local = down_weight[0]
    residual_local = residual[0]
    gain_full = norm_gain[0]
    qkv_local = qkv_weight[0]
    partial_sum = jnp.dot(hidden_local, down_local, preferred_element_type=jnp.float32)
    summed = lax.psum_scatter(partial_sum, "tensor", scatter_dimension=1, tiled=True)
    stream = (residual_local.astype(jnp.float32) + summed).astype(jnp.bfloat16)
    received = shifted(stream, "section", 1)
    gathered = lax.all_gather(received, "tensor", axis=1, tiled=True)
    normed = normalize(gathered.astype(jnp.float32), gain_full)
    projected = jnp.dot(normed, qkv_local, preferred_element_type=jnp.float32).astype(jnp.bfloat16)
    return (received[None], projected[None])


def solution(mesh):
    placed = (
        P("section", "groups", "tensor"),
        P("section", "tensor", None),
        P("section", "groups", "tensor"),
        P("section", None),
        P("section", None, "tensor"),
    )
    return jax.shard_map(
        body,
        mesh=mesh,
        in_specs=placed,
        out_specs=(P("section", "groups", "tensor"), P("section", "groups", "tensor")),
        check_vma=False,
    )
```

profile of v0, /device:TPU:0, one launch (start us, length us, event | category | flops | bytes accessed | tf_op | source)
XLA Modules:
  0.0 490.5 jit_solution(3447809766854134224)
XLA Ops:
  7.2 0.0 copy-start
  7.2 0.0 reduce-scatter.2.cloned.1.call-start
  7.2 1.9 copy-done
  9.1 35.6 %fusion = f32[512,8192]{1,0:T(8,128)} fusion(bf16[1,3328,8192]{2,1,0:T(8,128)(2,1)} %param.6, bf16[1,512,3328]{2,1,0:T(8,128)(2,1)S(1)} %copy-done), kind=kOutput, calls=%fused_computation | convolution fusion | flops 27917287424 | bytes 74711040 | tf_op jit(solution)/shard_map/dot_general | solution.py:30
  44.7 0.0 copy-start.4
  44.7 0.0 copy-start.5
  44.7 0.0 reduce-scatter.2.cloned.1.call-update
  44.7 0.0 all-gather.2.cloned.1.call-start
  44.8 285.5 %reduce-scatter.2.cloned.1.call-done = f32[512,1024]{1,0:T(8,128)} async-done(((f32[512,8192]{1,0:T(8,128)}), f32[512,1024]{1,0:T(8,128)}) %reduce-scatter.2.cloned.1.call-update) | async-done | bytes 2097168 | tf_op jit(solution)/shard_map/reduce_scatter | solution.py:31
  330.3 0.0 copy-done.4
  330.3 1.9 fusion.21
  332.2 0.1 collective-permute-start
  332.3 2.6 collective-permute-done
  334.9 0.0 copy-start.2
  334.9 1.0 copy-done.2
  335.9 0.0 all-gather.2.cloned.1.call-update
  335.9 124.1 %all-gather.2.cloned.1.call-done = bf16[512,8192]{1,0:T(8,128)(2,1)} async-done(((bf16[512,1024]{1,0:T(8,128)(2,1)}), bf16[512,8192]{1,0:T(8,128)(2,1)}) %all-gather.2.cloned.1.call-update) | async-done | bytes 8388624 | tf_op jit(solution)/shard_map/all_gather | solution.py:34
  460.0 5.1 %fusion.4 = f32[512]{0:T(512)S(1)} fusion(bf16[512,8192]{1,0:T(8,128)(2,1)} %all-gather.2.cloned.1.call-done), kind=kLoop, calls=%fused_computation.6 | loop fusion | flops 12582400 | bytes 8390656 | tf_op jit(solution)/shard_map/reduce_sum | solution.py:19
  465.1 0.0 copy-done.5
  465.1 0.0 copy-start.3
  465.1 0.0 copy-start.1
  465.2 17.5 %fusion.16 = bf16[1,512,1152]{2,1,0:T(8,128)(2,1)} fusion(bf16[1,8192,1152]{2,1,0:T(8,128)(2,1)} %param.9, bf16[512,8192]{1,0:T(8,128)(2,1)} %all-gather.2.cloned.1.call-done, f32[8192]{0:T(1024)S(1)} %bitcast.21, f32[512]{0:T(512)S(1)} %add_rsqrt_fusion), kind=kOutput, calls=%fused_computation.13 | convolution fusion | flops 9681043456 | bytes 28477440 | tf_op jit(solution)/shard_map/dot_general | solution.py:36
  482.6 0.0 copy-done.3
  482.6 1.0 copy.8
  483.6 0.0 copy-done.1
  (1 shorter events, 0.0 us)
Async XLA Ops:
  7.2 2.0 copy-start
  7.2 323.1 %reduce-scatter.2.cloned.1.call-start = ((), (), s32[]{:S(2)}) async-start(), calls=%async_computation.1 | async-start | bytes 18874368 | tf_op jit(solution)/shard_map/reduce_scatter | solution.py:31
  44.7 285.6 %copy-start.4 = (bf16[1,512,1024]{2,1,0:T(8,128)(2,1)S(1)}, bf16[1,512,1024]{2,1,0:T(8,128)(2,1)}, u32[]{:S(2)}) copy-start(bf16[1,512,1024]{2,1,0:T(8,128)(2,1)} %param.7) | copy-start | bytes 3145732
  44.7 420.4 %copy-start.5 = (f32[1,8192]{1,0:T(1,128)S(1)}, f32[1,8192]{1,0:T(1,128)}, u32[]{:S(2)}) copy-start(f32[1,8192]{1,0:T(1,128)} %param.8) | copy-start | bytes 98308
  44.7 415.3 %all-gather.2.cloned.1.call-start = ((), (), s32[]{:S(2)}) async-start(), calls=%async_computation.2 | async-start | bytes 9437184 | tf_op jit(solution)/shard_map/all_gather | solution.py:34
  332.2 2.7 collective-permute-start
  334.9 1.0 copy-start.2
  465.1 17.5 %copy-start.3 = (bf16[512,1024]{1,0:T(8,128)(2,1)S(1)}, bf16[512,1024]{1,0:T(8,128)(2,1)}, u32[]{:S(2)}) copy-start(bf16[512,1024]{1,0:T(8,128)(2,1)} %copy-done.2) | copy-start | bytes 3145732
  465.1 18.5 %copy-start.1 = (bf16[1,512,3328]{2,1,0:T(8,128)(2,1)S(1)}, bf16[1,512,3328]{2,1,0:T(8,128)(2,1)}, u32[]{:S(2)}) copy-start(bf16[1,512,3328]{2,1,0:T(8,128)(2,1)} %param.5) | copy-start | bytes 10223620
Sparse Core Ops, SparseCore 0:
  44.9 285.3 reduce-scatter.1
  336.1 123.9 all-gather.1
where the time goes:
time: 491 us; the launch traced here: 490 us
  waiting for transfers between devices  412 us (84%)
  matrix products  53 us (11%)
  between operations  14.1 us (3%)
  other arithmetic  7.05 us (1%)
    reduce_scatter x1, waiting for transfers between devices, body(): lax.psum_scatter(partial_sum, 'tensor', scatter_dimension=1, tiled=True)  285 us
    all_gather x1, waiting for transfers between devices, body(): gathered = lax.all_gather(received, 'tensor', axis=1, tiled=True)  124 us
    dot_general x1, matrix products, body(): jnp.dot(hidden_local, down_local, preferred_element_type=jnp.float32)  35.6 us
    dot_general x1, matrix products, body(): jnp.dot(normed, qkv_local, preferred_element_type=jnp.float32)  17.5 us
  transfers between devices with their start and end apart: 3, of which 3 were waited for; matrix products, arithmetic and copies ran while one was open for 0% of the time, Pallas kernels for 0%

commit v1 on v0

v1 whole, which is shorter than its diff:
```python
import functools

import jax
import jax.numpy as jnp
from jax import lax
from jax.experimental import pallas as pl
from jax.experimental.pallas import tpu as pltpu
from jax.sharding import PartitionSpec as P

epsilon = 1e-05
MESH = pl.DeviceIdType.MESH
PIECES = 2
BUFFERS = 4


def ring_order(n):
    inner = 1
    while inner * inner * 4 <= n:
        inner *= 2
    outer = n // inner
    if outer * inner != n or inner < 2 or outer % 2:
        return list(range(n))
    order = []
    for a in range(outer):
        columns = range(1, inner) if a % 2 == 0 else range(inner - 1, 0, -1)
        order += [a * inner + b for b in columns]
    return order + [a * inner for a in range(outer - 1, -1, -1)]


def lookup(table, index):
    found = jnp.int32(table[0])
    for k in range(1, len(table)):
        found = jnp.where(index == k, jnp.int32(table[k]), found)
    return found


def kernel(n, sections, hidden, down, residual, gain, qkv, received, projected,
           w_buf, q_buf, part, rs, ag, acc, square, w_sem, q_sem, rs_send, rs_recv,
           ag_send, ag_recv, swap_send, swap_recv):
    order = ring_order(n)
    position = [order.index(k) for k in range(n)]
    half, chunk = part.shape[1:]
    width = w_buf.shape[2]
    tiles = chunk // width
    rows = half // PIECES
    total_tiles = n * 2 * tiles

    me = lax.axis_index("tensor")
    here = lookup(position, me)
    at = lambda p: lookup(order, lax.rem(p + 2 * n, n))
    right, left = at(here + 1), at(here - 1)
    section = lax.axis_index("section")
    after = lax.rem(section + 1, sections)
    before = lax.rem(section + sections - 1, sections)
    towards = (right, left)

    def owner(s, d):
        return at(here - s) if d == 0 else at(here + s)

    def fetch(t):
        s = lax.div(t, 2 * tiles)
        d = lax.rem(lax.div(t, tiles), 2)
        j = lax.rem(t, tiles)
        c = at(here + (2 * d - 1) * (s + 1))
        start = pl.multiple_of(c * chunk + j * width, width)
        b = lax.rem(t, BUFFERS)
        return pltpu.make_async_copy(down.at[:, pl.ds(start, width)], w_buf.at[b], w_sem.at[b])

    for t in range(min(BUFFERS, total_tiles)):
        fetch(jnp.int32(t)).start()

    barrier = pltpu.get_barrier_semaphore()
    pl.semaphore_signal(barrier, inc=1, device_id={"tensor": left}, device_id_type=MESH)
    pl.semaphore_signal(barrier, inc=1, device_id={"tensor": right}, device_id_type=MESH)
    pl.semaphore_signal(barrier, inc=1, device_id={"section": before}, device_id_type=MESH)
    pl.semaphore_wait(barrier, 3)

    def span(piece):
        return pl.ds(piece * rows, rows)

    def rs_copy(s, d, piece):
        return pltpu.make_async_remote_copy(
            src_ref=rs.at[s, d, span(piece)],
            dst_ref=rs.at[s + 1, d, span(piece)],
            send_sem=rs_send.at[d, piece, lax.rem(s, 2)],
            recv_sem=rs_recv.at[d, piece, s],
            device_id={"tensor": towards[d]}, device_id_type=MESH)

    def swap_copy(d, piece):
        return pltpu.make_async_remote_copy(
            src_ref=rs.at[n - 1, d, span(piece)],
            dst_ref=ag.at[me, d, span(piece)],
            send_sem=swap_send.at[d, piece],
            recv_sem=swap_recv.at[d, piece],
            device_id={"section": after}, device_id_type=MESH)

    def ag_copy(s, d, piece, slot):
        return pltpu.make_async_remote_copy(
            src_ref=ag.at[slot, d, span(piece)],
            dst_ref=ag.at[slot, d, span(piece)],
            send_sem=ag_send.at[d, piece, lax.rem(s, 2)],
            recv_sem=ag_recv.at[d, piece, s],
            device_id={"tensor": towards[d]}, device_id_type=MESH)

    def reduce_step(s, first, last):
        for d in range(2):
            def tile(j, carry):
                t = (s * 2 + d) * tiles + j
                fetch(t).wait()
                part[d, :, pl.ds(pl.multiple_of(j * width, width), width)] = jnp.dot(
                    hidden[pl.ds(d * half, half), :], w_buf[lax.rem(t, BUFFERS)],
                    preferred_element_type=jnp.float32)

                @pl.when(t + BUFFERS < total_tiles)
                def _():
                    fetch(t + BUFFERS).start()
                return carry
            lax.fori_loop(0, tiles, tile, 0)
        for piece in range(PIECES):
            for d in range(2):
                value = part[d, span(piece), :]
                if not first:
                    rs_copy(s - 1, d, piece).wait_recv()
                    value = value + rs[s, d, span(piece), :].astype(jnp.float32)
                if last:
                    value = value + residual[pl.ds(d * half + piece * rows, rows), :].astype(jnp.float32)
                rs[s, d, span(piece), :] = value.astype(jnp.bfloat16)
                if last:
                    swap_copy(d, piece).start()
                else:
                    @pl.when(s >= 2)
                    def _():
                        rs_copy(s - 2, d, piece).wait_send()
                    rs_copy(s, d, piece).start()

    reduce_step(jnp.int32(0), True, False)
    q_copy = pltpu.make_async_copy(qkv, q_buf, q_sem)
    q_copy.start()

    def middle(s, carry):
        reduce_step(s, False, False)
        return carry
    lax.fori_loop(1, n - 1, middle, 0)
    reduce_step(jnp.int32(n - 1), False, True)

    for piece in range(PIECES):
        for d in range(2):
            swap_copy(d, piece).wait_recv()
            ag_copy(jnp.int32(0), d, piece, me).start()
    q_copy.wait()

    def project(d, c, first):
        x = ag[c, d].astype(jnp.float32)
        own = jnp.sum(x * x, axis=1, keepdims=True)
        scaled = (x * gain[c]).astype(jnp.bfloat16)
        product = jnp.dot(scaled, q_buf[c], preferred_element_type=jnp.float32)
        if first:
            square[d] = own
            acc[d] = product
        else:
            square[d] += own
            acc[d] += product

    for d in range(2):
        received[pl.ds(d * half, half), :] = ag[me, d]
        project(d, me, True)

    def gather_step(s, last):
        for piece in range(PIECES):
            for d in range(2):
                slot = owner(s + 1, d)
                ag_copy(s, d, piece, slot).wait_recv()
                if not last:
                    @pl.when(s >= 1)
                    def _():
                        ag_copy(s - 1, d, piece, owner(s - 1, d)).wait_send()
                    ag_copy(s + 1, d, piece, slot).start()
        for d in range(2):
            project(d, owner(s + 1, d), False)

    def gather(s, carry):
        gather_step(s, False)
        return carry
    lax.fori_loop(0, n - 2, gather, 0)
    gather_step(jnp.int32(n - 2), True)

    for d in range(2):
        scale = lax.rsqrt(square[d] / (n * chunk) + epsilon)
        projected[pl.ds(d * half, half), :] = (acc[d] * scale).astype(jnp.bfloat16)

    for piece in range(PIECES):
        for d in range(2):
            swap_copy(d, piece).wait_send()
            for s in range(max(n - 3, 0), n - 1):
                rs_copy(jnp.int32(s), d, piece).wait_send()
                ag_copy(jnp.int32(s), d, piece, owner(s, d)).wait_send()


def body(n, sections, hidden, down_weight, residual, norm_gain, qkv_weight):
    tokens, units = hidden.shape[1:]
    chunk = residual.shape[2]
    columns = qkv_weight.shape[2]
    half = tokens // 2
    width = 256 if chunk % 256 == 0 else chunk
    bf16, f32 = jnp.bfloat16, jnp.float32
    vmem = pl.BlockSpec(memory_space=pltpu.VMEM)
    far = pl.BlockSpec(memory_space=pl.ANY)
    dma = pltpu.SemaphoreType.DMA
    features = n * chunk
    received, projected = pl.pallas_call(
        functools.partial(kernel, n, sections),
        out_shape=(jax.ShapeDtypeStruct((tokens, chunk), bf16),
                   jax.ShapeDtypeStruct((tokens, columns), bf16)),
        in_specs=[vmem, far, vmem, vmem, far],
        out_specs=(vmem, vmem),
        scratch_shapes=[
            pltpu.VMEM((BUFFERS, units, width), bf16),
            pltpu.VMEM((n, chunk, columns), bf16),
            pltpu.VMEM((2, half, chunk), f32),
            pltpu.VMEM((n, 2, half, chunk), bf16),
            pltpu.VMEM((n, 2, half, chunk), bf16),
            pltpu.VMEM((2, half, columns), f32),
            pltpu.VMEM((2, half, 1), f32),
            dma((BUFFERS,)), dma,
            dma((2, PIECES, 2)), dma((2, PIECES, n)),
            dma((2, PIECES, 2)), dma((2, PIECES, n)),
            dma((2, PIECES)), dma((2, PIECES)),
        ],
        compiler_params=pltpu.CompilerParams(
            collective_id=0, has_side_effects=True, vmem_limit_bytes=60 * 2 ** 20),
        cost_estimate=pl.CostEstimate(
            flops=2 * tokens * features * (units + columns),
            bytes_accessed=2 * features * (units + columns), transcendentals=0),
    )(hidden[0], down_weight[0], residual[0],
      norm_gain[0].reshape(n, 1, chunk), qkv_weight[0].reshape(n, chunk, columns))
    return (received[None], projected[None])


def solution(mesh):
    placed = (
        P("section", "groups", "tensor"),
        P("section", "tensor", None),
        P("section", "groups", "tensor"),
        P("section", None),
        P("section", None, "tensor"),
    )
    return jax.shard_map(
        functools.partial(body, mesh.shape["tensor"], mesh.shape["section"]),
        mesh=mesh,
        in_specs=placed,
        out_specs=(P("section", "groups", "tensor"), P("section", "groups", "tensor")),
        check_vma=False,
    )
```

time: 491 us -> 181 us (0.37)
  waiting for transfers between devices: 412 us -> 0 us
  Pallas kernels: 0 us -> 175 us
  matrix products: 53 us -> 0 us
  between operations: 14.1 us -> 0.64 us
  other arithmetic: 7.05 us -> 0 us
    reduce_scatter x1 -> x0, waiting for transfers between devices: 285 us -> none  [body(): lax.psum_scatter(partial_sum, 'tensor', scatter_dimension=1, tiled=True)]
    pallas_call x0 -> x1, Pallas kernels: none -> 175 us  [body(): pl.pallas_call(functools.partial(kernel, n, sections), out_shape=(jax.Sha...]
    all_gather x1 -> x0, waiting for transfers between devices: 124 us -> none  [body(): gathered = lax.all_gather(received, 'tensor', axis=1, tiled=True)]
    dot_general x2 -> x0, matrix products: 53 us -> none  [the longest x1 35.6 us: body(): jnp.dot(hidden_local, down_local, preferred_element_type=jnp.float32)]
    reduce_sum x1 -> x0, other arithmetic: 5.1 us -> none  [normalize(): square_sum = jnp.sum(floats * floats, axis=1, keepdims=True)]
  transfers between devices with their start and end apart: 3 -> 0, of which waited for: 3 -> 0; matrix products, arithmetic and copies ran while one was open for 0% -> 0% of each run, Pallas kernels for 0% -> 0%
where the time goes in v1:
time: 181 us
  Pallas kernels  175 us (97%)
  local copies, waits for them, and re-layouts  4.64 us (3%)
    pallas_call x1, Pallas kernels, body(): pl.pallas_call(functools.partial(kernel, n, sections), out_shape=(jax.Sha...  175 us
    unnamed x2, local copies, waits for them, and re-layouts  4.64 us

profile of v1, /device:TPU:0, one launch (start us, length us, event | category | flops | bytes accessed | tf_op | source)
XLA Modules:
  0.0 180.6 jit_solution(16942795607128735818)
XLA Ops:
  0.6 175.4 %shard_map.68 = (bf16[512,1024]{1,0:T(8,128)(2,1)}, bf16[512,1152]{1,0:T(8,128)(2,1)}) custom-call(bf16[512,3328]{1,0:T(8,128)(2,1)} %bitcast.11, bf16[3328,8192]{1,0:T(8,128)(2,1)} %bitcast.9, bf16[512,1024]{1,0:T(8,128)(2,1)} %bitcast.12, f32[8,1,1024]{2,1,0:T(1,128)} %bitcast.13, bf16[8,1024,1152]{2,1,0:T(8,128)(2,1)} %bitcast.10), custom_call_target="tpu_custom_call" | custom-call | flops 37580963840 | bytes 73400320 | tf_op jit(solution)/shard_map/pallas_call | solution.py:210
  176.0 2.3 %copy.9 = bf16[1,512,1024]{2,1,0:T(8,128)(2,1)} copy(bf16[1,512,1024]{2,1,0:T(8,128)(2,1)} %bitcast.8) | data formatting | bytes 2097152
  178.3 2.4 %copy.10 = bf16[1,512,1152]{2,1,0:T(8,128)(2,1)} copy(bf16[1,512,1152]{2,1,0:T(8,128)(2,1)} %bitcast.7) | data formatting | bytes 2359296

commit v2 on v1

--- a/solution.py
+++ b/solution.py
@@ -9,7 +9,7 @@
 
 epsilon = 1e-05
 MESH = pl.DeviceIdType.MESH
-PIECES = 2
+PIECES = 4
 BUFFERS = 4
 
 
@@ -39,7 +39,7 @@
            ag_send, ag_recv, swap_send, swap_recv):
     order = ring_order(n)
     position = [order.index(k) for k in range(n)]
-    half, chunk = part.shape[1:]
+    half, chunk = part.shape[2:]
     width = w_buf.shape[2]
     tiles = chunk // width
     rows = half // PIECES
@@ -102,51 +102,66 @@
             recv_sem=ag_recv.at[d, piece, s],
             device_id={"tensor": towards[d]}, device_id_type=MESH)
 
-    def reduce_step(s, first, last):
-        for d in range(2):
-            def tile(j, carry):
-                t = (s * 2 + d) * tiles + j
-                fetch(t).wait()
-                part[d, :, pl.ds(pl.multiple_of(j * width, width), width)] = jnp.dot(
-                    hidden[pl.ds(d * half, half), :], w_buf[lax.rem(t, BUFFERS)],
-                    preferred_element_type=jnp.float32)
-
-                @pl.when(t + BUFFERS < total_tiles)
-                def _():
-                    fetch(t + BUFFERS).start()
-                return carry
-            lax.fori_loop(0, tiles, tile, 0)
+    def multiply_some(s, first, last):
+        def one(i, carry):
+            d = lax.div(i, tiles)
+            j = lax.rem(i, tiles)
+            t = s * 2 * tiles + i
+            fetch(t).wait()
+            part[lax.rem(s, 2), d, :, pl.ds(pl.multiple_of(j * width, width), width)] = jnp.dot(
+                hidden[pl.ds(pl.multiple_of(d * half, half), half), :], w_buf[lax.rem(t, BUFFERS)],
+                preferred_element_type=jnp.float32)
+
+            @pl.when(t + BUFFERS < total_tiles)
+            def _():
+                fetch(t + BUFFERS).start()
+            return carry
+        lax.fori_loop(first, last, one, 0)
+
+    def combine(s, d, piece, first, last):
+        value = part[lax.rem(s, 2), d, span(piece), :]
+        if not first:
+            rs_copy(s - 1, d, piece).wait_recv()
+            value = value + rs[s, d, span(piece), :].astype(jnp.float32)
+        if last:
+            value = value + residual[pl.ds(d * half + piece * rows, rows), :].astype(jnp.float32)
+        rs[s, d, span(piece), :] = value.astype(jnp.bfloat16)
+        if last:
+            swap_copy(d, piece).start()
+        else:
+            @pl.when(s >= 2)
+            def _():
+                rs_copy(s - 2, d, piece).wait_send()
+            rs_copy(s, d, piece).start()
+
+    zero = jnp.int32(0)
+    for d in range(2):
+        multiply_some(zero, d * tiles, (d + 1) * tiles)
+        for piece in range(PIECES):
+            combine(zero, d, piece, True, False)
+    q_copy = pltpu.make_async_copy(qkv, q_buf, q_sem)
+    q_copy.start()
+    multiply_some(zero + 1, 0, 2 * tiles)
+
+    def middle(s, carry):
         for piece in range(PIECES):
             for d in range(2):
-                value = part[d, span(piece), :]
-                if not first:
-                    rs_copy(s - 1, d, piece).wait_recv()
-                    value = value + rs[s, d, span(piece), :].astype(jnp.float32)
-                if last:
-                    value = value + residual[pl.ds(d * half + piece * rows, rows), :].astype(jnp.float32)
-                rs[s, d, span(piece), :] = value.astype(jnp.bfloat16)
-                if last:
-                    swap_copy(d, piece).start()
-                else:
-                    @pl.when(s >= 2)
-                    def _():
-                        rs_copy(s - 2, d, piece).wait_send()
-                    rs_copy(s, d, piece).start()
-
-    reduce_step(jnp.int32(0), True, False)
-    q_copy = pltpu.make_async_copy(qkv, q_buf, q_sem)
-    q_copy.start()
-
-    def middle(s, carry):
-        reduce_step(s, False, False)
+                combine(s, d, piece, False, False)
+            multiply_some(s + 1, 2 * tiles * piece // PIECES, 2 * tiles * (piece + 1) // PIECES)
         return carry
     lax.fori_loop(1, n - 1, middle, 0)
-    reduce_step(jnp.int32(n - 1), False, True)
+
+    def begin_gather(piece):
+        for d in range(2):
+            swap_copy(d, piece).wait_recv()
+            ag_copy(zero, d, piece, me).start()
 
     for piece in range(PIECES):
         for d in range(2):
-            swap_copy(d, piece).wait_recv()
-            ag_copy(jnp.int32(0), d, piece, me).start()
+            combine(zero + n - 1, d, piece, False, True)
+        if piece:
+            begin_gather(piece - 1)
+    begin_gather(PIECES - 1)
     q_copy.wait()
 
     def project(d, c, first):
@@ -165,24 +180,27 @@
         received[pl.ds(d * half, half), :] = ag[me, d]
         project(d, me, True)
 
-    def gather_step(s, last):
+    def gather_step(s, first, last):
         for piece in range(PIECES):
             for d in range(2):
                 slot = owner(s + 1, d)
                 ag_copy(s, d, piece, slot).wait_recv()
                 if not last:
-                    @pl.when(s >= 1)
-                    def _():
+                    if not first:
                         ag_copy(s - 1, d, piece, owner(s - 1, d)).wait_send()
                     ag_copy(s + 1, d, piece, slot).start()
-        for d in range(2):
-            project(d, owner(s + 1, d), False)
+            if not first and piece in (0, PIECES // 2):
+                project(min(piece, 1), owner(s, min(piece, 1)), False)
+
+    gather_step(zero, True, False)
 
     def gather(s, carry):
-        gather_step(s, False)
+        gather_step(s, False, False)
         return carry
-    lax.fori_loop(0, n - 2, gather, 0)
-    gather_step(jnp.int32(n - 2), True)
+    lax.fori_loop(1, n - 2, gather, 0)
+    gather_step(zero + n - 2, False, True)
+    for d in range(2):
+        project(d, owner(n - 1, d), False)
 
     for d in range(2):
         scale = lax.rsqrt(square[d] / (n * chunk) + epsilon)
@@ -216,7 +234,7 @@
         scratch_shapes=[
             pltpu.VMEM((BUFFERS, units, width), bf16),
             pltpu.VMEM((n, chunk, columns), bf16),
-            pltpu.VMEM((2, half, chunk), f32),
+            pltpu.VMEM((2, 2, half, chunk), f32),
             pltpu.VMEM((n, 2, half, chunk), bf16),
             pltpu.VMEM((n, 2, half, chunk), bf16),
             pltpu.VMEM((2, half, columns), f32),

time: 181 us -> 180 us (level)
  no operation moved by 1% of the time
where the time goes in v2:
time: 180 us
  Pallas kernels  174 us (97%)
  local copies, waits for them, and re-layouts  4.64 us (3%)
    pallas_call x1, Pallas kernels, body(): pl.pallas_call(functools.partial(kernel, n, sections), out_shape=(jax.Sha...  174 us
    unnamed x2, local copies, waits for them, and re-layouts  4.64 us

profile of v2, /device:TPU:0, one launch (start us, length us, event | category | flops | bytes accessed | tf_op | source)
XLA Modules:
  0.0 179.7 jit_solution(11135181357275241688)
XLA Ops:
  0.6 174.4 %shard_map.68 = (bf16[512,1024]{1,0:T(8,128)(2,1)}, bf16[512,1152]{1,0:T(8,128)(2,1)}) custom-call(bf16[512,3328]{1,0:T(8,128)(2,1)} %bitcast.11, bf16[3328,8192]{1,0:T(8,128)(2,1)} %bitcast.9, bf16[512,1024]{1,0:T(8,128)(2,1)} %bitcast.12, f32[8,1,1024]{2,1,0:T(1,128)} %bitcast.13, bf16[8,1024,1152]{2,1,0:T(8,128)(2,1)} %bitcast.10), custom_call_target="tpu_custom_call" | custom-call | flops 37580963840 | bytes 73400320 | tf_op jit(solution)/shard_map/pallas_call | solution.py:228
  175.0 2.3 %copy.9 = bf16[1,512,1024]{2,1,0:T(8,128)(2,1)} copy(bf16[1,512,1024]{2,1,0:T(8,128)(2,1)} %bitcast.8) | data formatting | bytes 2097152
  177.3 2.4 %copy.10 = bf16[1,512,1152]{2,1,0:T(8,128)(2,1)} copy(bf16[1,512,1152]{2,1,0:T(8,128)(2,1)} %bitcast.7) | data formatting | bytes 2359296

commit v3 on v2

--- a/solution.py
+++ b/solution.py
@@ -34,8 +34,8 @@
     return found
 
 
-def kernel(n, sections, hidden, down, residual, gain, qkv, received, projected,
-           w_buf, q_buf, part, rs, ag, acc, square, w_sem, q_sem, rs_send, rs_recv,
+def kernel(n, sections, hidden_far, down, residual_far, gain, qkv, received, projected,
+           hidden, residual, w_buf, q_buf, part, rs, ag, acc, square, w_sem, q_sem, in_sem, rs_send, rs_recv,
            ag_send, ag_recv, swap_send, swap_recv):
     order = ring_order(n)
     position = [order.index(k) for k in range(n)]
@@ -66,6 +66,9 @@
         b = lax.rem(t, BUFFERS)
         return pltpu.make_async_copy(down.at[:, pl.ds(start, width)], w_buf.at[b], w_sem.at[b])
 
+    hidden_copy = pltpu.make_async_copy(hidden_far, hidden, in_sem.at[0])
+    residual_copy = pltpu.make_async_copy(residual_far, residual, in_sem.at[1])
+    hidden_copy.start()
     for t in range(min(BUFFERS, total_tiles)):
         fetch(jnp.int32(t)).start()
 
@@ -135,12 +138,14 @@
             rs_copy(s, d, piece).start()
 
     zero = jnp.int32(0)
+    hidden_copy.wait()
     for d in range(2):
         multiply_some(zero, d * tiles, (d + 1) * tiles)
         for piece in range(PIECES):
             combine(zero, d, piece, True, False)
     q_copy = pltpu.make_async_copy(qkv, q_buf, q_sem)
     q_copy.start()
+    residual_copy.start()
     multiply_some(zero + 1, 0, 2 * tiles)
 
     def middle(s, carry):
@@ -156,6 +161,7 @@
             swap_copy(d, piece).wait_recv()
             ag_copy(zero, d, piece, me).start()
 
+    residual_copy.wait()
     for piece in range(PIECES):
         for d in range(2):
             combine(zero + n - 1, d, piece, False, True)
@@ -176,8 +182,10 @@
             square[d] += own
             acc[d] += product
 
+    own_copies = [pltpu.make_async_copy(ag.at[me, d], received.at[pl.ds(d * half, half)], in_sem.at[d])
+                  for d in range(2)]
     for d in range(2):
-        received[pl.ds(d * half, half), :] = ag[me, d]
+        own_copies[d].start()
         project(d, me, True)
 
     def gather_step(s, first, last):
@@ -203,6 +211,7 @@
         project(d, owner(n - 1, d), False)
 
     for d in range(2):
+        own_copies[d].wait()
         scale = lax.rsqrt(square[d] / (n * chunk) + epsilon)
         projected[pl.ds(d * half, half), :] = (acc[d] * scale).astype(jnp.bfloat16)
 
@@ -212,6 +221,19 @@
             for s in range(max(n - 3, 0), n - 1):
                 rs_copy(jnp.int32(s), d, piece).wait_send()
                 ag_copy(jnp.int32(s), d, piece, owner(s, d)).wait_send()
+
+
+def hand_on(received_in, projected_in, received, projected, sems):
+    half = received_in.shape[0] // 2
+    copies = []
+    for k, (source, target) in enumerate(((received_in, received), (projected_in, projected))):
+        for d in range(2):
+            part = pl.ds(d * half, half)
+            copies.append(pltpu.make_async_copy(source.at[part], target.at[part], sems.at[k, d]))
+    for copy in copies:
+        copy.start()
+    for copy in copies:
+        copy.wait()
 
 
 def body(n, sections, hidden, down_weight, residual, norm_gain, qkv_weight):
@@ -229,9 +251,11 @@
         functools.partial(kernel, n, sections),
         out_shape=(jax.ShapeDtypeStruct((tokens, chunk), bf16),
                    jax.ShapeDtypeStruct((tokens, columns), bf16)),
-        in_specs=[vmem, far, vmem, vmem, far],
-        out_specs=(vmem, vmem),
+        in_specs=[far, far, far, vmem, far],
+        out_specs=(far, vmem),
         scratch_shapes=[
+            pltpu.VMEM((tokens, units), bf16),
+            pltpu.VMEM((tokens, chunk), bf16),
             pltpu.VMEM((BUFFERS, units, width), bf16),
             pltpu.VMEM((n, chunk, columns), bf16),
             pltpu.VMEM((2, 2, half, chunk), f32),
@@ -239,7 +263,7 @@
             pltpu.VMEM((n, 2, half, chunk), bf16),
             pltpu.VMEM((2, half, columns), f32),
             pltpu.VMEM((2, half, 1), f32),
-            dma((BUFFERS,)), dma,
+            dma((BUFFERS,)), dma, dma((2,)),
             dma((2, PIECES, 2)), dma((2, PIECES, n)),
             dma((2, PIECES, 2)), dma((2, PIECES, n)),
             dma((2, PIECES)), dma((2, PIECES)),
@@ -251,6 +275,14 @@
             bytes_accessed=2 * features * (units + columns), transcendentals=0),
     )(hidden[0], down_weight[0], residual[0],
       norm_gain[0].reshape(n, 1, chunk), qkv_weight[0].reshape(n, chunk, columns))
+    received, projected = pl.pallas_call(
+        hand_on,
+        out_shape=(jax.ShapeDtypeStruct((tokens, chunk), bf16),
+                   jax.ShapeDtypeStruct((tokens, columns), bf16)),
+        in_specs=[vmem, vmem],
+        out_specs=(far, far),
+        scratch_shapes=[dma((2, 2))],
+    )(received, projected)
     return (received[None], projected[None])
 
 

time: 180 us -> 179 us (level)
  local copies, waits for them, and re-layouts: 4.64 us -> 0 us
  Pallas kernels: 174 us -> 178 us
    unnamed x2 -> x0, local copies, waits for them, and re-layouts: 4.64 us -> none
    pallas_call x0 -> x1, Pallas kernels: none -> 2.98 us  [body(): pl.pallas_call(hand_on, out_shape=(jax.ShapeDtypeStruct((tokens, chunk),...]
where the time goes in v3:
time: 179 us; the launch traced here: 178 us
  Pallas kernels  178 us (99%)
    pallas_call x1, Pallas kernels, body(): pl.pallas_call(functools.partial(kernel, n, sections), out_shape=(jax.Sha...  175 us

profile of v3, /device:TPU:0, one launch (start us, length us, event | category | flops | bytes accessed | tf_op | source)
XLA Modules:
  0.0 178.4 jit_solution(8393576754297958375)
XLA Ops:
  0.6 174.8 %shard_map.68 = (bf16[512,1024]{1,0:T(8,128)(2,1)}, bf16[512,1152]{1,0:T(8,128)(2,1)}) custom-call(bf16[512,3328]{1,0:T(8,128)(2,1)} %bitcast.9, bf16[3328,8192]{1,0:T(8,128)(2,1)} %bitcast.7, bf16[512,1024]{1,0:T(8,128)(2,1)} %bitcast.11, f32[8,1,1024]{2,1,0:T(1,128)} %bitcast.13, bf16[8,1024,1152]{2,1,0:T(8,128)(2,1)} %bitcast.8), custom_call_target="tpu_custom_call" | custom-call | flops 37580963840 | bytes 73400320 | tf_op jit(solution)/shard_map/pallas_call | solution.py:250
  175.5 3.0 %shard_map.69 = (bf16[512,1024]{1,0:T(8,128)(2,1)}, bf16[512,1152]{1,0:T(8,128)(2,1)}) custom-call(bf16[512,1024]{1,0:T(8,128)(2,1)} %get-tuple-element.6.received_in, bf16[512,1152]{1,0:T(8,128)(2,1)} %get-tuple-element.7.projected_in), custom_call_target="tpu_custom_call" | custom-call | tf_op jit(solution)/shard_map/pallas_call | solution.py:278

commit v4 on v3

--- a/solution.py
+++ b/solution.py
@@ -9,7 +9,7 @@
 
 epsilon = 1e-05
 MESH = pl.DeviceIdType.MESH
-PIECES = 4
+PIECES = 2
 BUFFERS = 4
 
 

time: 179 us -> 180 us (level)
  no operation moved by 1% of the time
where the time goes in v4:
time: 180 us
  Pallas kernels  179 us (99%)
    pallas_call x1, Pallas kernels, body(): pl.pallas_call(functools.partial(kernel, n, sections), out_shape=(jax.Sha...  176 us

profile of v4, /device:TPU:0, one launch (start us, length us, event | category | flops | bytes accessed | tf_op | source)
XLA Modules:
  0.0 180.1 jit_solution(14818901929136749228)
XLA Ops:
  0.6 176.5 %shard_map.68 = (bf16[512,1024]{1,0:T(8,128)(2,1)}, bf16[512,1152]{1,0:T(8,128)(2,1)}) custom-call(bf16[512,3328]{1,0:T(8,128)(2,1)} %bitcast.9, bf16[3328,8192]{1,0:T(8,128)(2,1)} %bitcast.7, bf16[512,1024]{1,0:T(8,128)(2,1)} %bitcast.11, f32[8,1,1024]{2,1,0:T(1,128)} %bitcast.13, bf16[8,1024,1152]{2,1,0:T(8,128)(2,1)} %bitcast.8), custom_call_target="tpu_custom_call" | custom-call | flops 37580963840 | bytes 73400320 | tf_op jit(solution)/shard_map/pallas_call | solution.py:250
  177.1 3.0 %shard_map.69 = (bf16[512,1024]{1,0:T(8,128)(2,1)}, bf16[512,1152]{1,0:T(8,128)(2,1)}) custom-call(bf16[512,1024]{1,0:T(8,128)(2,1)} %get-tuple-element.6.received_in, bf16[512,1152]{1,0:T(8,128)(2,1)} %get-tuple-element.7.projected_in), custom_call_target="tpu_custom_call" | custom-call | tf_op jit(solution)/shard_map/pallas_call | solution.py:278
